TPU v7x, 512 devices: a whole 4x8x8 slice. The times are simulated.
512 devices in a mesh: seq: 32 (over x, z), users: 16 (over y, core).
Axes of the slice: x: 4, y: 8, z: 8, core: 2. Of those that a mesh axis runs over, the one named last changes fastest.
Arguments:
- cand_items: int32 [4096, 2], P(('users', 'seq')), parts along dimension 0, may hold values from 0 to 127
- item_rows: bfloat16 [2048, 1024], P('users'), parts along dimension 0
- hist_keys: bfloat16 [32, 16384, 1024], P('users', 'seq'), parts along dimension 0, may hold values from -6 to 6
- hist_values: bfloat16 [32, 16384, 1024], P('users', 'seq'), parts along dimension 0
- block_mask: int32 [32, 2, 128], P('users', None, 'seq'), parts along dimension 0, may hold values 0 or 1
- hist_lengths: int32 [32], P('users'), parts along dimension 0, may hold values from 4096 to 16384, as said below
- gain_in: float32 [1024], replicated, may hold values from 0.1 to 1.9
- w_query: bfloat16 [1024, 1024], P('seq'), may hold values from -0.1875 to 0.1875
- w_gate: bfloat16 [1024, 1024], P('seq'), may hold values from -0.1875 to 0.1875
- gain_attn: float32 [1024], replicated, may hold values from 0.1 to 1.9
- w_out: bfloat16 [1024, 1024], P('seq'), may hold values from -0.1875 to 0.1875
Outputs:
- ranked: bfloat16 [4096, 2, 1024], P(('users', 'seq')), parts along dimension 0
There are 16 independent parts, one for each index of `users`. A program takes and returns all parts, laid end to end along the dimension named above; an argument that names none is the same for every part. Nothing has to cross between parts.
Inputs may be any that keep to these rules, and one draw needn't show every extreme that they name: `hist_lengths`: in every group at least one user has all 16384 history events valid.
All inputs are finite; a program needn't handle non-finite values. No bound on the sum of `block_mask` on one device may be relied on, other than what follows from the above.
Results may differ from a plain program's by a relative error of at most 0.012.
Values may be sent and summed in bfloat16 or wider, within the bound.
A program may use at most 64 MiB of HBM per device.

v0:
```python
import math

import jax
import jax.numpy as jnp
from jax import lax
from jax.sharding import PartitionSpec as P

HEADS = 8
HEAD_DIM = 128
TILE = 128
BLOCK = 128


EPSILON = 1e-06


def scaled_rows(values, gain):
    wide = values.astype(jnp.float32)
    return wide * lax.rsqrt(jnp.mean(wide * wide, axis=-1, keepdims=True) + EPSILON) * gain


def on_device(
    cand_items,
    item_rows,
    hist_keys,
    hist_values,
    block_mask,
    hist_lengths,
    gain_in,
    w_query,
    w_gate,
    gain_attn,
    w_out,
):
    row_count, user_count = cand_items.shape
    model_width = item_rows.shape[1]
    head_width = model_width // HEADS
    event_count = hist_keys.shape[1]
    block_count = event_count // BLOCK
    tile_count = block_mask.shape[1]
    seq_index = lax.axis_index("seq")
    own_count = row_count * user_count
    score_scale = HEAD_DIM ** (-0.5)
    positions = seq_index * event_count + jnp.arange(event_count, dtype=jnp.int32)
    tokens = item_rows[cand_items]
    own_normed = scaled_rows(tokens, gain_in).astype(jnp.bfloat16).reshape(own_count, model_width)
    columns = own_normed
    query_pre = jnp.dot(
        columns,
        lax.all_gather(w_query, "seq", axis=0, tiled=True),
        preferred_element_type=jnp.float32,
    )
    gate_pre = jnp.dot(
        columns,
        lax.all_gather(w_gate, "seq", axis=0, tiled=True),
        preferred_element_type=jnp.float32,
    )
    query_own = (
        jax.nn.silu(query_pre).astype(jnp.bfloat16).reshape(row_count, user_count, model_width)
    )
    query_all = lax.all_gather(query_own, "seq", axis=0, tiled=True)
    gate = jax.nn.silu(gate_pre).astype(jnp.bfloat16).reshape(row_count, user_count, model_width)
    event_open = jnp.where(positions[None, :] < hist_lengths[:, None], 1.0, 0.0).astype(jnp.float32)
    event_open = event_open.reshape(user_count, block_count, BLOCK)
    row_total = lax.axis_size("seq") * row_count
    row_tile = jnp.arange(row_total, dtype=jnp.int32) // TILE
    tile_onehot = (row_tile[:, None] == jnp.arange(tile_count, dtype=jnp.int32)[None, :]).astype(
        jnp.int32
    )
    outputs = []
    for user_index in range(user_count):
        row_open = jnp.sum(tile_onehot[:, :, None] * block_mask[user_index][None], axis=1)
        keys_user = hist_keys[user_index].reshape(event_count, HEADS, head_width)
        values_user = hist_values[user_index].reshape(event_count, HEADS, head_width)
        open_user = event_open[user_index]
        row_step = math.gcd(row_total, 512)
        query_blocks = query_all[:, user_index].reshape(
            row_total // row_step, row_step, HEADS, head_width
        )
        open_blocks = row_open.reshape(row_total // row_step, row_step, block_count)

        def dense_rows(operands):
            query_block, open_rows = operands
            scores = (
                jnp.einsum(
                    "chd,ehd->hce", query_block, keys_user, preferred_element_type=jnp.float32
                )
                * score_scale
            )
            keep = open_rows.astype(jnp.float32)[:, :, None] * open_user[None]
            weights = (jax.nn.silu(scores) * keep.reshape(row_step, event_count)[None]).astype(
                jnp.bfloat16
            )
            return jnp.einsum(
                "hce,ehd->chd", weights, values_user, preferred_element_type=jnp.float32
            )

        result = lax.map(dense_rows, (query_blocks, open_blocks))
        outputs.append(result.reshape(row_total, model_width))
    attended = lax.psum_scatter(
        jnp.stack(outputs, axis=1).astype(jnp.bfloat16), "seq", scatter_dimension=0, tiled=True
    ).astype(jnp.float32)
    mixed = (scaled_rows(attended, gain_attn) * gate.astype(jnp.float32)).astype(jnp.bfloat16)
    mixed = mixed.reshape(own_count, model_width)
    columns = mixed
    projected = jnp.dot(
        columns,
        lax.all_gather(w_out, "seq", axis=0, tiled=True),
        preferred_element_type=jnp.float32,
    )
    return (
        tokens.astype(jnp.float32) + projected.reshape(row_count, user_count, model_width)
    ).astype(jnp.bfloat16)


def solution(mesh):
    in_specs = (
        P(("users", "seq"), None),
        P("users", None),
        P("users", "seq", None),
        P("users", "seq", None),
        P("users", None, "seq"),
        P("users"),
        P(),
        P("seq", None),
        P("seq", None),
        P(),
        P("seq", None),
    )
    out_specs = P(("users", "seq"), None, None)
    return jax.shard_map(
        on_device, mesh=mesh, in_specs=in_specs, out_specs=out_specs, check_vma=False
    )
```

profile of v0, /device:TPU:56, one launch (start us, length us, event | category | flops | bytes accessed | tf_op | source)
XLA Modules:
  0.0 580.9 jit_solution(7025906957369672534)
XLA Ops:
  6.5 0.0 copy-start
  6.5 0.0 all-gather.5.cloned.1.call-start
  6.5 0.7 all-gather.5.cloned.1.call-update
  7.3 0.0 all-gather.7.cloned.1.call-start
  7.3 0.7 compare_select_fusion.1
  8.0 0.1 copy.71
  8.1 0.1 reshape.147
  8.2 0.0 copy-done
  8.2 0.6 gather_fusion
  8.8 0.1 multiply_reduce_fusion
  8.9 0.1 rsqrt.20
  9.0 89.5 %all-gather.5.cloned.1.call-done = bf16[1024,1024]{1,0:T(8,128)(2,1)} async-done(((bf16[32,1024]{1,0:T(8,128)(2,1)}), bf16[1024,1024]{1,0:T(8,128)(2,1)}) %all-gather.5.cloned.1.call-update) | async-done | bytes 2097168 | tf_op jit(solution)/shard_map/all_gather | solution.py:50
  98.6 2.0 multiply_convert_fusion.3
  100.6 0.6 reshape.142
  101.3 0.0 all-gather.7.cloned.1.call-update
  101.3 0.0 all-gather.9.cloned.1.call-start
  101.3 0.7 all-gather.9.cloned.1.call-update
  102.0 0.0 reduce-scatter.4.cloned.1.call-start
  102.1 0.0 copy-done.6
  102.1 0.1 multiply_reduce_fusion.2
  102.2 0.8 copy.76
  103.0 1.7 fusion.26
  104.7 1.3 copy.98
  106.0 1.7 fusion.27
  107.7 1.3 copy.77
  109.1 0.1 copy.82
  109.2 0.0 copy-start.7
  109.3 0.0 copy-start.3
  109.3 1.3 copy.83
  110.6 1.3 copy.100
  111.9 0.0 copy-done.7
  111.9 0.1 compare_select_fusion
  112.0 0.0 copy-done.3
  112.0 0.3 mul.188
  112.3 0.9 bitcast_multiply_fusion.1
  113.2 0.3 mul.200
  113.5 0.8 bitcast_multiply_fusion
  114.4 66.4 %all-gather.7.cloned.1.call-done = bf16[256,2,1024]{2,1,0:T(2,128)(2,1)} async-done(((bf16[8,2,1024]{2,1,0:T(2,128)(2,1)}), bf16[256,2,1024]{2,1,0:T(2,128)(2,1)}) %all-gather.7.cloned.1.call-update) | async-done | bytes 1048592 | tf_op jit(solution)/shard_map/all_gather | solution.py:61
  180.8 3.3 fusion.28
  184.1 2.0 copy.97
  186.1 0.0 copy-done.1
  186.1 4.5 fusion.5
  190.6 1.3 copy.84
  191.9 0.9 copy.99
  192.9 0.0 copy-done.2
  192.9 3.6 fusion.4
  196.5 0.2 copy.85
  196.7 0.1 maximum_bitcast_fusion
  196.8 0.0 copy-start.4
  196.8 1.1 copy.101
  197.9 0.0 reduce-scatter.4.cloned.1.call-update
  197.9 0.0 all-gather.11.cloned.1.call-start
  197.9 0.5 all-gather.11.cloned.1.call-update
  198.5 66.8 %all-gather.9.cloned.1.call-done = bf16[1024,1024]{1,0:T(8,128)(2,1)} async-done(((bf16[32,1024]{1,0:T(8,128)(2,1)}), bf16[1024,1024]{1,0:T(8,128)(2,1)}) %all-gather.9.cloned.1.call-update) | async-done | bytes 2097168 | tf_op jit(solution)/shard_map/all_gather | solution.py:55
  265.3 0.0 copy-done.4
  265.3 2.0 fusion.16
  267.3 219.5 %reduce-scatter.4.cloned.1.call-done = bf16[8,2048]{1,0:T(8,128)(2,1)} async-done(((bf16[256,2048]{1,0:T(8,128)(2,1)}), bf16[8,2048]{1,0:T(8,128)(2,1)}) %reduce-scatter.4.cloned.1.call-update) | async-done | bytes 32784
  486.9 0.9 fusion.12
  487.7 0.1 copy.86
  487.8 0.1 copy.87
  487.9 83.8 %all-gather.11.cloned.1.call-done = bf16[1024,1024]{1,0:T(8,128)(2,1)} async-done(((bf16[32,1024]{1,0:T(8,128)(2,1)}), bf16[1024,1024]{1,0:T(8,128)(2,1)}) %all-gather.11.cloned.1.call-update) | async-done | bytes 2097168 | tf_op jit(solution)/shard_map/all_gather | solution.py:108
  571.7 0.0 copy-done.5
  571.7 2.0 fusion.9
  573.7 0.7 copy.90
  (16 shorter events, 0.1 us)
Async XLA Ops:
  6.5 1.6 copy-start
  6.5 95.5 %copy-start.6 = (s32[2,2,4]{2,1,0:T(2,128)S(1)}, s32[2,2,4]{2,1,0:T(2,128)}, u32[]{:S(2)}) copy-start(s32[2,2,4]{2,1,0:T(2,128)} %param.15) | copy-start | bytes 196
  6.5 92.0 %all-gather.5.cloned.1.call-start = ((), (), s32[]{:S(2)}) async-start(), calls=%async_computation.1 | async-start | bytes 2162688 | tf_op jit(solution)/shard_map/all_gather | solution.py:50
  7.3 173.5 %all-gather.7.cloned.1.call-start = ((), (), s32[]{:S(2)}) async-start(), calls=%async_computation.2 | async-start | bytes 1081344 | tf_op jit(solution)/shard_map/all_gather | solution.py:61
  101.3 164.0 %all-gather.9.cloned.1.call-start = ((), (), s32[]{:S(2)}) async-start(), calls=%async_computation.3 | async-start | bytes 2162688 | tf_op jit(solution)/shard_map/all_gather | solution.py:55
  102.0 384.9 %reduce-scatter.4.cloned.1.call-start = ((), (), s32[]{:S(2)}) async-start(), calls=%async_computation.5 | async-start | bytes 1081344
  109.2 2.7 copy-start.7
  109.3 2.7 copy-start.3
  114.4 71.7 %copy-start.1 = (bf16[1,512,1024]{1,2,0:T(8,128)(2,1)S(1)}, bf16[1,512,1024]{1,2,0:T(8,128)(2,1)}, u32[]{:S(2)}) copy-start(bf16[1,512,1024]{1,2,0:T(8,128)(2,1)} %copy.98) | copy-start | bytes 3145732
  190.6 2.3 copy-start.2
  196.8 68.5 %copy-start.4 = (f32[1024]{0:T(1024)S(1)}, f32[1024]{0:T(1024)}, u32[]{:S(2)}) copy-start(f32[1024]{0:T(1024)} %param.17) | copy-start | bytes 12292
  197.9 373.8 %copy-start.5 = (f32[1024]{0:T(1024)S(1)}, f32[1024]{0:T(1024)}, u32[]{:S(2)}) copy-start(f32[1024]{0:T(1024)} %param.20) | copy-start | bytes 12292
  197.9 373.8 %all-gather.11.cloned.1.call-start = ((), (), s32[]{:S(2)}) async-start(), calls=%async_computation.4 | async-start | bytes 2162688 | tf_op jit(solution)/shard_map/all_gather | solution.py:108
Sparse Core Ops, SparseCore 0:
  10.5 87.9 all-gather.4
  101.7 79.0 all-gather.6
  184.0 81.2 all-gather.8
  269.5 217.3 reduce-scatter.3
  489.9 81.7 all-gather.10
where the time goes:
time: 582 us; the launch traced here: 581 us
  waiting for transfers between devices  528 us (91%)
  local copies, waits for them, and re-layouts  21.5 us (4%)
  matrix products  14.2 us (2%)
  between operations  13.3 us (2%)
    unnamed x6, waiting for transfers between devices  221 us
    all_gather x1, waiting for transfers between devices, on_device(): lax.all_gather(w_query, 'seq', axis=0, tiled=True)  89.5 us
    all_gather x1, waiting for transfers between devices, on_device(): lax.all_gather(w_out, 'seq', axis=0, tiled=True)  83.8 us
    all_gather x1, waiting for transfers between devices, on_device(): lax.all_gather(w_gate, 'seq', axis=0, tiled=True)  66.8 us
    all_gather x1, waiting for transfers between devices, on_device(): query_all = lax.all_gather(query_own, 'seq', axis=0, tiled=True)  66.4 us
  transfers between devices with their start and end apart: 5, of which 5 were waited for; matrix products, arithmetic and copies ran while one was open for 6% of the time, Pallas kernels for 0%

commit v1 on v0

v1 whole, which is shorter than its diff:
```python
import jax
import jax.numpy as jnp
from jax import lax
from jax.experimental import pallas as pl
from jax.experimental.pallas import tpu as pltpu
from jax.sharding import PartitionSpec as P

HEADS = 8
HEAD_DIM = 128
BLOCK = 128
EPSILON = 1e-06
XS, ZS = 4, 8
NEAREST = (7, 1, 6, 2, 5, 3, 4)
MESH = pl.DeviceIdType.MESH
BF16, F32 = jnp.bfloat16, jnp.float32


def silu(v):
    return v / (1.0 + jnp.exp(-v))


def push(src, dst, send_sem, recv_sem, seq):
    return pltpu.make_async_remote_copy(
        src_ref=src, dst_ref=dst, send_sem=send_sem, recv_sem=recv_sem,
        device_id={"seq": seq}, device_id_type=MESH)


def kernel(
    cand, items_hbm, keys_hbm, vals_hbm, mask, lens, gain_in, wq_hbm, wg_hbm, gain_attn, wo_hbm,
    out,
    items, keys, vals, normed, picks, ids_x, chooser, live, tokens, wq, wg, wo_rows, wo, query, gate,
    part, part_in, half, half_in, proj, proj_in, sq, sq_in,
    load_sem, wq_zs, wq_zr, wq_xs, wq_xr, wg_zs, wg_zr, wg_xs, wg_xr, oh_zs, oh_zr, oh_xs, oh_xr,
    wo_xs, wo_xr, wo_zs, wo_zr, q_s, q_r, rx_s, rx_r, rz_s, rz_r, po_s, po_r, sq_s, sq_r,
):
    me = lax.axis_index("seq")
    x, z = lax.div(me, ZS), lax.rem(me, ZS)
    rows = wq_hbm.shape[0]
    own = picks.shape[1]
    users, events = keys_hbm.shape[0], keys_hbm.shape[1]
    item_count = items_hbm.shape[0]

    def z_at(step):
        return lax.rem(z + step + ZS, ZS)

    def x_at(step):
        return lax.rem(x + step + XS, XS)

    def lanes(index):
        return pl.ds(pl.multiple_of(index * HEAD_DIM, HEAD_DIM), HEAD_DIM)

    def rows_of(seq):
        return pl.ds(pl.multiple_of(seq * rows, rows), rows)

    barrier = pltpu.get_barrier_semaphore()
    for j in range(1, ZS):
        pl.semaphore_signal(barrier, inc=1, device_id={"seq": x * ZS + z_at(j)}, device_id_type=MESH)
    for j in range(1, XS):
        pl.semaphore_signal(barrier, inc=1, device_id={"seq": x_at(j) * ZS + z}, device_id_type=MESH)

    loads = [
        pltpu.make_async_copy(items_hbm, items, load_sem.at[0]),
        pltpu.make_async_copy(wq_hbm.at[:, lanes(z)], wq.at[rows_of(me)], load_sem.at[1]),
        pltpu.make_async_copy(wg_hbm.at[:, lanes(z)], wg.at[rows_of(me)], load_sem.at[2]),
        pltpu.make_async_copy(wo_hbm, wo_rows.at[x], load_sem.at[3]),
    ]
    for u in range(users):
        loads.append(pltpu.make_async_copy(keys_hbm.at[u], keys.at[u], load_sem.at[4 + 2 * u]))
        loads.append(pltpu.make_async_copy(vals_hbm.at[u], vals.at[u], load_sem.at[5 + 2 * u]))
    for load in loads:
        load.start()

    row = lax.broadcasted_iota(jnp.int32, (own, own // users), 0)
    column = lax.broadcasted_iota(jnp.int32, (own, own // users), 1)
    ids = jnp.zeros((own, 1), F32)
    for u in range(users):
        here = row == column * users + u
        ids += jnp.sum(
            jnp.where(here, cand[u : u + 1, :].astype(F32), 0.0), axis=1, keepdims=True)
    item = lax.broadcasted_iota(jnp.int32, (own, item_count), 1).astype(F32)
    own_pick = jnp.where(item == ids, 1.0, 0.0).astype(BF16)
    picks[z] = own_pick

    pl.semaphore_wait(barrier, XS + ZS - 2)

    sends = []

    def send(copy):
        copy.start()
        sends.append(copy)

    for j in range(1, ZS):
        to = z_at(j)
        send(push(wq_hbm.at[:, lanes(to)], wq.at[rows_of(me)], wq_zs.at[j], wq_zr.at[j], x * ZS + to))
    for j in range(1, XS):
        send(push(wo_hbm, wo_rows.at[x], wo_xs.at[j], wo_xr.at[j], x_at(j) * ZS + z))

    loads[0].wait()
    wide = items[...].astype(F32)
    normed[...] = (
        wide * lax.rsqrt(jnp.mean(wide * wide, axis=-1, keepdims=True) + EPSILON) * gain_in[...]
    ).astype(BF16)

    def group(at):
        return pl.ds(pl.multiple_of(at * (ZS * rows), ZS * rows), ZS * rows)

    def widen(buf, zr, xs, xr):
        for j in range(1, ZS):
            come = buf.at[rows_of(x * ZS + z_at(-j))]
            push(come, come, zr.at[j], zr.at[j], me).wait_recv()
        for j in range(1, XS):
            send(push(buf.at[group(x)], buf.at[group(x)], xs.at[j], xr.at[j], x_at(j) * ZS + z))

    loads[1].wait()
    widen(wq, wq_zr, wq_xs, wq_xr)

    for j in range(1, ZS):
        to = z_at(j)
        send(push(picks.at[z], picks.at[z], oh_zs.at[j], oh_zr.at[j], x * ZS + to))
    for j in range(1, ZS):
        to = z_at(j)
        send(push(wg_hbm.at[:, lanes(to)], wg.at[rows_of(me)], wg_zs.at[j], wg_zr.at[j], x * ZS + to))

    tokens[...] = jnp.dot(own_pick, items[...], preferred_element_type=F32)
    tiles = mask.shape[1]
    for u in range(users):
        length = lens[u] - me * events
        for t in range(tiles):
            for b in range(events // BLOCK):
                place = b * BLOCK + lax.broadcasted_iota(jnp.int32, (1, BLOCK), 1)
                opened = jnp.full((1, BLOCK), mask[u, t, b], jnp.int32)
                live[pl.ds(u * tiles + t, 1), pl.ds(b * BLOCK, BLOCK)] = jnp.where(
                    (opened == 1) & (place < length), 1.0, 0.0)

    for j in range(1, XS):
        come = wq.at[group(x_at(-j))]
        push(come, come, wq_xr.at[j], wq_xr.at[j], me).wait_recv()
    query[z] = silu(jnp.dot(normed[...], wq[...], preferred_element_type=F32)).astype(BF16)
    for j in NEAREST:
        send(push(query.at[z], query.at[z], q_s.at[j], q_r.at[j], x * ZS + z_at(j)))

    for j in range(1, ZS):
        come = picks.at[z_at(-j)]
        push(come, come, oh_zr.at[j], oh_zr.at[j], me).wait_recv()
    group_rows = ZS * own
    picked = picks[...].reshape(group_rows, item_count)
    number = lax.broadcasted_iota(jnp.int32, (own, item_count), 1).astype(F32).astype(BF16)
    ids_x[x] = lax.dot_general(
        number, picked, (((1,), (1,)), ((), ())), preferred_element_type=F32).astype(BF16)
    for j in range(1, XS):
        send(push(ids_x.at[x], ids_x.at[x], oh_xs.at[j], oh_xr.at[j], x_at(j) * ZS + z))

    loads[2].wait()
    widen(wg, wg_zr, wg_xs, wg_xr)

    for j in range(1, XS):
        come = ids_x.at[x_at(-j)]
        push(come, come, oh_xr.at[j], oh_xr.at[j], me).wait_recv()
    user_of = lax.rem(lax.broadcasted_iota(jnp.int32, (group_rows, item_count), 0), users)
    down = lax.broadcasted_iota(jnp.int32, (item_count, group_rows), 0).astype(F32)
    per_tile = XS // tiles
    for s in range(XS):
        chosen = jnp.transpose(jnp.where(down == ids_x[s, 0:1, :].astype(F32), 1.0, 0.0))
        for u in range(users):
            chooser[s // per_tile, pl.ds(s % per_tile * group_rows, group_rows),
                    pl.ds(u * item_count, item_count)] = jnp.where(
                        user_of == u, chosen, 0.0).astype(BF16)

    per_head = HEAD_DIM // rows
    slot = lax.rem(z, per_head)
    place_wo = pl.ds(pl.multiple_of(slot * rows, rows), rows)
    heads_x = ZS // per_head

    def spread_wo():
        for j in range(1, XS):
            come = wo_rows.at[x_at(-j)]
            push(come, come, wo_xr.at[j], wo_xr.at[j], me).wait_recv()
        loads[3].wait()
        for s in range(XS):
            to = s * heads_x + lax.div(z, per_head)
            copy = push(wo_rows.at[s], wo.at[place_wo], wo_zs.at[s], wo_zr.at[slot], x * ZS + to)

            @pl.when(to != z)
            def _():
                copy.start()

            @pl.when(to == z)
            def _():
                wo[place_wo] = wo_rows[s]

    def make_gate():
        for j in range(1, XS):
            come = wg.at[group(x_at(-j))]
            push(come, come, wg_xr.at[j], wg_xr.at[j], me).wait_recv()
        gate_items = silu(jnp.dot(normed[...], wg[...], preferred_element_type=F32)).astype(BF16)
        rows_x = picks[...].reshape(group_rows, item_count)
        gate[...] = jnp.dot(rows_x, gate_items, preferred_element_type=F32) * gain_attn[:, lanes(z)]

    for load in loads[4:]:
        load.wait()

    lag = 2

    def head_of(k):
        flip = 1 - 2 * lax.rem(k + 1, 2)
        return lax.rem(z + flip * lax.div(k + 1, 2) + ZS, ZS)

    def attend(k):
        h = head_of(k)
        j = lax.rem(z - h + ZS, ZS)

        @pl.when(k > 0)
        def _():
            push(query.at[h], query.at[h], q_r.at[j], q_r.at[j], me).wait_recv()

        asked = query[h]
        sums = []
        for u in range(users):
            scores = lax.dot_general(
                asked, keys[u, :, lanes(h)], (((1,), (1,)), ((), ())), preferred_element_type=F32)
            halved = scores * (0.5 * HEAD_DIM ** (-0.5))
            weight = halved + halved * jnp.tanh(halved)
            kept = jnp.concatenate(
                [weight * live[pl.ds(u * tiles + t, 1), :] for t in range(tiles)], axis=0)
            sums.append(jnp.dot(
                kept.astype(BF16), vals[u, :, lanes(h)], preferred_element_type=F32).astype(BF16))
        for t in range(tiles):
            both = jnp.concatenate(
                [s[t * item_count : (t + 1) * item_count] for s in sums], axis=0)
            sel = jnp.dot(chooser[t], both, preferred_element_type=F32).astype(BF16)
            for i in range(XS // tiles):
                part[h, t * (XS // tiles) + i] = sel[i * group_rows : (i + 1) * group_rows]
        for j in range(1, XS):
            to = x_at(j)
            push(part.at[h, to], part_in.at[h, x], rx_s.at[k * XS + j], rx_r.at[k * XS + j],
                 to * ZS + z).start()

    def reduce_x(k):
        h = head_of(k)
        total = part[h, x].astype(F32)
        for j in range(1, XS):
            come = part_in.at[h, x_at(-j)]
            push(come, come, rx_r.at[k * XS + j], rx_r.at[k * XS + j], me).wait_recv()
            total += part_in[h, x_at(-j)].astype(F32)
        half[h] = total.astype(BF16)

        @pl.when(k > 0)
        def _():
            j = lax.rem(h - z + ZS, ZS)
            push(half.at[h], half_in.at[z], rz_s.at[j], rz_r.at[j], x * ZS + h).start()

    def step(k, carry):
        @pl.when(k < HEADS)
        def _():
            attend(k)

        @pl.when(k == HEADS // 2)
        def _():
            spread_wo()

        @pl.when(k == HEADS)
        def _():
            make_gate()

        @pl.when(k >= lag)
        def _():
            reduce_x(k - lag)

        return carry

    lax.fori_loop(0, HEADS + lag, step, 0)

    for i in range(per_head):
        frm = per_head * lax.rem(z, heads_x) + i

        @pl.when(frm != z)
        def _():
            come = wo.at[pl.ds(i * rows, rows)]
            push(come, come, wo_zr.at[i], wo_zr.at[i], me).wait_recv()

    attended = half[z].astype(F32)
    for j in range(1, ZS):
        come = half_in.at[z_at(-j)]
        push(come, come, rz_r.at[j], rz_r.at[j], me).wait_recv()
        attended += half_in[z_at(-j)].astype(F32)
    sq[...] = (attended * attended).reshape(sq.shape)
    for j in range(1, ZS):
        to = z_at(j)
        send(push(sq.at[to], sq_in.at[z], sq_s.at[j], sq_r.at[j], x * ZS + to))
    proj[...] = jnp.dot(
        (attended * gate[...]).astype(BF16), wo[...], preferred_element_type=F32
    ).astype(BF16).reshape(proj.shape)
    for j in range(1, ZS):
        to = z_at(j)
        send(push(proj.at[to], proj_in.at[z], po_s.at[j], po_r.at[j], x * ZS + to))

    squares = sq[z]
    for j in range(1, ZS):
        come = sq_in.at[z_at(-j)]
        push(come, come, sq_r.at[j], sq_r.at[j], me).wait_recv()
        squares += sq_in[z_at(-j)]
    scale = lax.rsqrt(jnp.sum(squares, axis=1, keepdims=True) * (1.0 / (HEADS * HEAD_DIM)) + EPSILON)
    projected = proj[z].astype(F32)
    for j in range(1, ZS):
        come = proj_in.at[z_at(-j)]
        push(come, come, po_r.at[j], po_r.at[j], me).wait_recv()
        projected += proj_in[z_at(-j)].astype(F32)
    out[...] = (tokens[...] + projected * scale).astype(BF16)

    for copy in sends:
        copy.wait_send()
    for s in range(XS):
        to = s * heads_x + lax.div(z, per_head)

        @pl.when(to != z)
        def _():
            push(wo_rows.at[s], wo.at[place_wo], wo_zs.at[s], wo_zr.at[slot], x * ZS + to).wait_send()

    def drain(k, carry):
        for j in range(1, XS):
            gone = part.at[head_of(k), x_at(j)]
            push(gone, gone, rx_s.at[k * XS + j], rx_r.at[k * XS + j], me).wait_send()
        return carry

    lax.fori_loop(0, HEADS, drain, 0)
    for j in range(1, ZS):
        gone = half.at[z_at(j)]
        push(gone, gone, rz_s.at[j], rz_r.at[j], me).wait_send()


def on_device(
    cand_items, item_rows, hist_keys, hist_values, block_mask, hist_lengths,
    gain_in, w_query, w_gate, gain_attn, w_out,
):
    row_count, users = cand_items.shape
    item_count, width = item_rows.shape
    events = hist_keys.shape[1]
    rows = w_query.shape[0]
    own = row_count * users
    tiles = block_mask.shape[1]
    group_rows = ZS * own
    dma = pltpu.SemaphoreType.DMA
    anywhere = pl.BlockSpec(memory_space=pl.ANY)
    vmem = pl.BlockSpec(memory_space=pltpu.VMEM)
    smem = pl.BlockSpec(memory_space=pltpu.SMEM)
    ranked = pl.pallas_call(
        kernel,
        out_shape=jax.ShapeDtypeStruct((own, width), BF16),
        in_specs=[vmem, anywhere, anywhere, anywhere, smem, smem, vmem, anywhere, anywhere, vmem, anywhere],
        out_specs=vmem,
        scratch_shapes=[
            pltpu.VMEM((item_count, width), BF16),
            pltpu.VMEM((users, events, width), BF16),
            pltpu.VMEM((users, events, width), BF16),
            pltpu.VMEM((item_count, width), BF16),
            pltpu.VMEM((ZS, own, item_count), BF16),
            pltpu.VMEM((XS, own, group_rows), BF16),
            pltpu.VMEM((tiles, XS * ZS // tiles * own, users * item_count), BF16),
            pltpu.VMEM((users * tiles, events), F32),
            pltpu.VMEM((own, width), F32),
            pltpu.VMEM((XS * ZS * rows, HEAD_DIM), BF16),
            pltpu.VMEM((XS * ZS * rows, HEAD_DIM), BF16),
            pltpu.VMEM((XS, rows, width), BF16),
            pltpu.VMEM((HEAD_DIM, width), BF16),
            pltpu.VMEM((HEADS, item_count, HEAD_DIM), BF16),
            pltpu.VMEM((group_rows, HEAD_DIM), F32),
            pltpu.VMEM((HEADS, XS, group_rows, HEAD_DIM), BF16),
            pltpu.VMEM((HEADS, XS, group_rows, HEAD_DIM), BF16),
            pltpu.VMEM((HEADS, group_rows, HEAD_DIM), BF16),
            pltpu.VMEM((ZS, group_rows, HEAD_DIM), BF16),
            pltpu.VMEM((ZS, own, width), BF16),
            pltpu.VMEM((ZS, own, width), BF16),
            pltpu.VMEM((ZS, own, HEAD_DIM), F32),
            pltpu.VMEM((ZS, own, HEAD_DIM), F32),
            dma((4 + 2 * users,)),
            dma((ZS,)), dma((ZS,)), dma((XS,)), dma((XS,)),
            dma((ZS,)), dma((ZS,)), dma((XS,)), dma((XS,)),
            dma((ZS,)), dma((ZS,)), dma((XS,)), dma((XS,)),
            dma((XS,)), dma((XS,)), dma((XS,)), dma((HEAD_DIM // rows,)),
            dma((ZS,)), dma((ZS,)),
            dma((HEADS * XS,)), dma((HEADS * XS,)),
            dma((ZS,)), dma((ZS,)),
            dma((ZS,)), dma((ZS,)),
            dma((ZS,)), dma((ZS,)),
        ],
        compiler_params=pltpu.CompilerParams(
            collective_id=0, has_side_effects=True, vmem_limit_bytes=63 * 1024 * 1024),
        cost_estimate=pl.CostEstimate(flops=10**9, bytes_accessed=5 * 10**6, transcendentals=10**6),
        name="ranked",
    )(
        cand_items.T, item_rows, hist_keys, hist_values, block_mask, hist_lengths,
        gain_in.reshape(1, width), w_query, w_gate, gain_attn.reshape(1, width), w_out,
    )
    return ranked.reshape(row_count, users, width)


def solution(mesh):
    in_specs = (
        P(("users", "seq"), None),
        P("users", None),
        P("users", "seq", None),
        P("users", "seq", None),
        P("users", None, "seq"),
        P("users"),
        P(),
        P("seq", None),
        P("seq", None),
        P(),
        P("seq", None),
    )
    out_specs = P(("users", "seq"), None, None)
    return jax.shard_map(
        on_device, mesh=mesh, in_specs=in_specs, out_specs=out_specs, check_vma=False
    )
```

time: 582 us -> 59.4 us (0.10)
  waiting for transfers between devices: 528 us -> 0 us
  Pallas kernels: 0 us -> 57.7 us
  local copies, waits for them, and re-layouts: 21.5 us -> 1.39 us
  matrix products: 14.2 us -> 0 us
  between operations: 13.3 us -> 0.01 us
    all_gather x4 -> x0, waiting for transfers between devices: 307 us -> none  [the longest x1 89.5 us: on_device(): lax.all_gather(w_query, 'seq', axis=0, tiled=True)]
    unnamed x6 -> x0, waiting for transfers between devices: 221 us -> none
    pallas_call x0 -> x1, Pallas kernels: none -> 57.7 us  [on_device(): pl.pallas_call(kernel, out_shape=jax.ShapeDtypeStruct((own, width), BF16)...]
    dot_general x5 -> x0, matrix products: 14.2 us -> none  [the longest x2 8.11 us: dense_rows(): jnp.einsum('hce,ehd->chd', weights, values_user, preferred_element_type=j...]
    slice x6 -> x0, local copies, waits for them, and re-layouts: 9.37 us -> none  [the longest x3 4.39 us: on_device(): hist_values[user_index].reshape(event_count, HEADS, head_width)]
    unnamed x21 -> x0, local copies, waits for them, and re-layouts: 6.65 us -> none
  transfers between devices with their start and end apart: 5 -> 0, of which waited for: 5 -> 0; matrix products, arithmetic and copies ran while one was open for 6% -> 0% of each run, Pallas kernels for 0% -> 0%
where the time goes in v1:
time: 59.4 us; the launch traced here: 59.1 us
  Pallas kernels  57.7 us (97%)
  local copies, waits for them, and re-layouts  1.39 us (2%)
    pallas_call x1, Pallas kernels, on_device(): pl.pallas_call(kernel, out_shape=jax.ShapeDtypeStruct((own, width), BF16)...  57.7 us
    reshape x1, local copies, waits for them, and re-layouts, on_device(): return ranked.reshape(row_count, users, width)  1.39 us

profile of v1, /device:TPU:56, one launch (start us, length us, event | category | flops | bytes accessed | tf_op | source)
XLA Modules:
  0.0 59.1 jit_solution(16530432702149109876)
XLA Ops:
  0.0 57.7 %ranked.1 = bf16[16,1024]{1,0:T(8,128)(2,1)} custom-call(s32[2,8]{1,0:T(2,128)} %bitcast.5, bf16[128,1024]{1,0:T(8,128)(2,1)} %items_hbm.1, bf16[2,512,1024]{2,1,0:T(8,128)(2,1)} %keys_hbm.1, bf16[2,512,1024]{2,1,0:T(8,128)(2,1)} %vals_hbm.1, s32[2,2,4]{2,1,0:T(2,128)} %mask.1, s32[2]{0:T(128)} %lens.1, f32[1,1024]{1,0:T(1,128)} %bitcast.3, ...), custom_call_target="tpu_custom_call" | custom-call | flops 1000000000 | bytes 5000000 | tf_op jit(solution)/shard_map/ranked/pallas_call | solution.py:346
  57.7 1.4 %reshape.11 = bf16[8,2,1024]{2,1,0:T(2,128)(2,1)} reshape(bf16[16,1024]{1,0:T(8,128)(2,1)} %ranked.1) | data formatting | bytes 65536 | tf_op jit(solution)/shard_map/reshape | solution.py:394

commit v2 on v1

v2 whole, which is shorter than its diff:
```python
import jax
import jax.numpy as jnp
from jax import lax
from jax.experimental import pallas as pl
from jax.experimental.pallas import tpu as pltpu
from jax.sharding import PartitionSpec as P

HEADS = 8
HEAD_DIM = 128
BLOCK = 128
EPSILON = 1e-06
XS, ZS = 4, 8
NEAREST = (7, 1, 6, 2, 5, 3, 4)
TEAM = 4
MESH = pl.DeviceIdType.MESH
BF16, F32 = jnp.bfloat16, jnp.float32


def silu(v):
    return v / (1.0 + jnp.exp(-v))


def push(src, dst, send_sem, recv_sem, seq):
    return pltpu.make_async_remote_copy(
        src_ref=src, dst_ref=dst, send_sem=send_sem, recv_sem=recv_sem,
        device_id={"seq": seq}, device_id_type=MESH)


def kernel(
    cand_hbm, items_hbm, keys_hbm, vals_hbm, mask_hbm, lens_hbm, gain_in_hbm, wq_hbm, wg_hbm,
    gain_attn_hbm, wo_hbm,
    out,
    cand, mask, lens, gain_in, gain_attn, items, keys, vals, normed, picks, ids_x, chooser, live,
    tokens, wq, wg, wo, query, gate_out, gate_in, part, part_in, half, half_in, proj, proj_in, sq, sq_in,
    load_sem, wq_zs, wq_zr, wq_xs, wq_xr, wg_zs, wg_zr, wg_xs, wg_xr, oh_zs, oh_zr, oh_xs, oh_xr,
    wo_zs, wo_zr, wo_ts, wo_tr, q_s, q_r, ga_s, ga_r, rx_s, rx_r, rz_s, rz_r, po_s, po_r, sq_s, sq_r,
):
    me = lax.axis_index("seq")
    x, z = lax.div(me, ZS), lax.rem(me, ZS)
    team = min(TEAM, lax.axis_size("users"))
    member = lax.rem(lax.axis_index("users"), team)
    team_at = lax.axis_index("users") - member
    rows = wq_hbm.shape[0]
    own = picks.shape[1]
    tiles = mask.shape[1]
    users, events = keys_hbm.shape[0], keys_hbm.shape[1]
    item_count = items_hbm.shape[0]

    def z_at(step):
        return lax.rem(z + step + ZS, ZS)

    def x_at(step):
        return lax.rem(x + step + XS, XS)

    def lanes(index):
        return pl.ds(pl.multiple_of(index * HEAD_DIM, HEAD_DIM), HEAD_DIM)

    def rows_of(seq):
        return pl.ds(pl.multiple_of(seq * rows, rows), rows)

    share = wo_hbm.shape[1] // team

    def share_of(at):
        return pl.ds(pl.multiple_of(at * share, share), share)

    def mate(step):
        return lax.rem(member + step, team)

    barrier = pltpu.get_barrier_semaphore()
    for j in range(1, ZS):
        pl.semaphore_signal(barrier, inc=1, device_id={"seq": x * ZS + z_at(j)}, device_id_type=MESH)
    for j in range(1, XS):
        pl.semaphore_signal(barrier, inc=1, device_id={"seq": x_at(j) * ZS + z}, device_id_type=MESH)

    for j in range(1, team):
        pl.semaphore_signal(barrier, inc=1, device_id={"users": team_at + mate(j)}, device_id_type=MESH)

    loads = [
        pltpu.make_async_copy(cand_hbm, cand, load_sem.at[0]),
        pltpu.make_async_copy(items_hbm, items, load_sem.at[1]),
        pltpu.make_async_copy(gain_in_hbm, gain_in, load_sem.at[2]),
        pltpu.make_async_copy(wq_hbm.at[:, lanes(z)], wq.at[rows_of(me)], load_sem.at[3]),
        pltpu.make_async_copy(wg_hbm.at[:, lanes(z)], wg.at[rows_of(me)], load_sem.at[4]),
        pltpu.make_async_copy(
            wo_hbm.at[:, share_of(member)], wo.at[rows_of(z), share_of(member)], load_sem.at[5]),
        pltpu.make_async_copy(gain_attn_hbm, gain_attn, load_sem.at[6]),
        pltpu.make_async_copy(mask_hbm, mask, load_sem.at[7]),
        pltpu.make_async_copy(lens_hbm, lens, load_sem.at[8]),
    ]
    for u in range(users):
        loads.append(pltpu.make_async_copy(keys_hbm.at[u], keys.at[u], load_sem.at[9 + 2 * u]))
        loads.append(pltpu.make_async_copy(vals_hbm.at[u], vals.at[u], load_sem.at[10 + 2 * u]))
    for load in loads[:4]:
        load.start()

    pl.semaphore_wait(barrier, XS + ZS + team - 3)

    sends = []

    def send(copy):
        copy.start()
        sends.append(copy)

    for j in range(1, ZS):
        to = z_at(j)
        send(push(wq_hbm.at[:, lanes(to)], wq.at[rows_of(me)], wq_zs.at[j], wq_zr.at[j], x * ZS + to))
    for load in loads[4:]:
        load.start()

    loads[0].wait()
    each = own // users
    row = lax.broadcasted_iota(jnp.int32, (own, each), 0)
    column = lax.broadcasted_iota(jnp.int32, (own, each), 1)
    ids = jnp.zeros((own, 1), F32)
    for u in range(users):
        here = row == column + u * each
        ids += jnp.sum(
            jnp.where(here, cand[u : u + 1, :].astype(F32), 0.0), axis=1, keepdims=True)
    item = lax.broadcasted_iota(jnp.int32, (own, item_count), 1).astype(F32)
    own_pick = jnp.where(item == ids, 1.0, 0.0).astype(BF16)
    picks[z] = own_pick

    for j in range(1, ZS):
        send(push(picks.at[z], picks.at[z], oh_zs.at[j], oh_zr.at[j], x * ZS + z_at(j)))

    loads[1].wait()
    loads[2].wait()
    wide = items[...].astype(F32)
    normed[...] = (
        wide * lax.rsqrt(jnp.mean(wide * wide, axis=-1, keepdims=True) + EPSILON) * gain_in[...]
    ).astype(BF16)

    def group(at):
        return pl.ds(pl.multiple_of(at * (ZS * rows), ZS * rows), ZS * rows)

    loads[3].wait()
    for j in range(1, ZS):
        come = wq.at[rows_of(x * ZS + z_at(-j))]
        push(come, come, wq_zr.at[j], wq_zr.at[j], me).wait_recv()
    for j in range(1, XS):
        send(push(wq.at[group(x)], wq.at[group(x)], wq_xs.at[j], wq_xr.at[j], x_at(j) * ZS + z))

    for j in range(1, ZS):
        to = z_at(j)
        send(push(wg_hbm.at[:, lanes(to)], wg.at[rows_of(me)], wg_zs.at[j], wg_zr.at[j], x * ZS + to))

    for j in range(1, ZS):
        come = picks.at[z_at(-j)]
        push(come, come, oh_zr.at[j], oh_zr.at[j], me).wait_recv()
    group_rows = ZS * own
    picked = picks[...].reshape(group_rows, item_count)
    number = lax.broadcasted_iota(jnp.int32, (own, item_count), 1).astype(F32).astype(BF16)
    ids_x[x] = lax.dot_general(
        number, picked, (((1,), (1,)), ((), ())), preferred_element_type=F32).astype(BF16)
    for j in range(1, XS):
        send(push(ids_x.at[x], ids_x.at[x], oh_xs.at[j], oh_xr.at[j], x_at(j) * ZS + z))

    tokens[...] = jnp.dot(own_pick, items[...], preferred_element_type=F32)
    loads[7].wait()
    loads[8].wait()
    for u in range(users):
        length = lens[u] - me * events
        for t in range(tiles):
            for b in range(events // BLOCK):
                place = b * BLOCK + lax.broadcasted_iota(jnp.int32, (1, BLOCK), 1)
                opened = jnp.full((1, BLOCK), mask[u, t, b], jnp.int32)
                live[u * tiles + t, :, pl.ds(b * BLOCK, BLOCK)] = jnp.where(
                    (opened == 1) & (place < length), 1.0, 0.0)

    for j in range(1, XS):
        come = wq.at[group(x_at(-j))]
        push(come, come, wq_xr.at[j], wq_xr.at[j], me).wait_recv()
    query[z] = silu(jnp.dot(normed[...], wq[...], preferred_element_type=F32)).astype(BF16)
    for j in NEAREST:
        send(push(query.at[z], query.at[z], q_s.at[j], q_r.at[j], x * ZS + z_at(j)))

    gate_x = lax.div(z, HEADS // XS)
    gate_step = lax.rem(gate_x - x + XS, XS)
    wg_copy = push(wg.at[group(x)], wg.at[group(x)], wg_xs.at[gate_step], wg_xr.at[gate_step],
                   gate_x * ZS + z)
    slot = lax.rem(z, HEADS // XS)
    loads[4].wait()
    for j in range(1, ZS):
        come = wg.at[rows_of(x * ZS + z_at(-j))]
        push(come, come, wg_zr.at[j], wg_zr.at[j], me).wait_recv()

    @pl.when(gate_x != x)
    def _():
        wg_copy.start()

    for j in range(1, ZS):
        send(push(wo_hbm.at[:, share_of(member)], wo.at[rows_of(z), share_of(member)],
                  wo_zs.at[j], wo_zr.at[j], x * ZS + z_at(j)))

    def share_copy(j):
        return pltpu.make_async_remote_copy(
            src_ref=wo.at[:, share_of(member)], dst_ref=wo.at[:, share_of(member)],
            send_sem=wo_ts.at[j], recv_sem=wo_tr.at[j],
            device_id={"users": team_at + mate(j)}, device_id_type=MESH)

    def share_wo():
        loads[5].wait()
        for j in range(1, ZS):
            come = wo.at[rows_of(z_at(-j)), share_of(member)]
            push(come, come, wo_zr.at[j], wo_zr.at[j], me).wait_recv()
        for j in range(1, team):
            share_copy(j).start()

    for j in range(1, XS):
        come = ids_x.at[x_at(-j)]
        push(come, come, oh_xr.at[j], oh_xr.at[j], me).wait_recv()
    down = lax.broadcasted_iota(jnp.int32, (item_count, group_rows), 0).astype(F32)
    per_tile = XS // tiles
    user_rows = XS * ZS * each
    z_rows = XS * each
    shown = []
    for s in range(XS):
        chosen = jnp.transpose(jnp.where(down == ids_x[s, 0:1, :].astype(F32), 1.0, 0.0))
        shown.append(chosen.reshape(ZS, own, item_count))
    blank = jnp.zeros((ZS, each, item_count), F32)
    for u in range(users):
        wide_rows = []
        for s in range(XS):
            mine = shown[s][:, u * each : (u + 1) * each]
            wide_rows.append(jnp.concatenate(
                [mine if t == s // per_tile else blank for t in range(tiles)], axis=2))
        chooser[u] = jnp.concatenate(wide_rows, axis=1).reshape(
            user_rows, tiles * item_count).astype(BF16)

    def gate_copy(j):
        to = z_at(j)
        return push(gate_out.at[to], gate_in.at[slot], ga_s.at[j], ga_r.at[slot], x * ZS + to)

    def make_gate():
        for j in range(1, XS):
            come = wg.at[group(x_at(-j))]
            push(come, come, wg_xr.at[j], wg_xr.at[j], me).wait_recv()
        gate_items = silu(jnp.dot(normed[...], wg[...], preferred_element_type=F32)).astype(BF16)
        twice = jnp.concatenate([gate_items] * tiles, axis=0)
        for u in range(users):
            gate_out[:, u] = jnp.dot(
                chooser[u], twice, preferred_element_type=F32
            ).astype(BF16).reshape(ZS, z_rows, HEAD_DIM)
        for j in NEAREST[::-1]:
            gate_copy(j).start()
        gate_in[slot] = gate_out[z]

    for load in loads[9:]:
        load.wait()

    pairs = HEADS // 2
    steps = users * pairs

    def place_of(k):
        u, s = lax.div(k, pairs), lax.rem(k, pairs)
        early = lax.div(z, 2) + s + lax.div(s, 2) * (5 - 2 * s)
        late = x + 1 + s
        first = jnp.where(u == 0, 1, 0)
        return u, lax.rem(first * early + (1 - first) * late + 2 * pairs, pairs)

    def part_copy(u, p):
        j = lax.rem(p - x + XS, XS)
        return push(part.at[u, p], part_in.at[u, x], rx_s.at[u * XS + j], rx_r.at[u * XS + j],
                    p * ZS + z)

    def attend(k):
        u, p = place_of(k)
        heads = (2 * p, 2 * p + 1)

        for h in heads:
            @pl.when((k < pairs) & (h != z))
            def _():
                j = lax.rem(z - h + ZS, ZS)
                push(query.at[h], query.at[h], q_r.at[j], q_r.at[j], me).wait_recv()

        nothing = jnp.zeros((item_count, HEAD_DIM), BF16)
        asked = jnp.concatenate([
            jnp.concatenate([query[heads[0]], nothing], axis=1),
            jnp.concatenate([nothing, query[heads[1]]], axis=1)], axis=0)
        columns = pl.ds(pl.multiple_of(p * 2 * HEAD_DIM, 2 * HEAD_DIM), 2 * HEAD_DIM)
        scores = lax.dot_general(
            asked, keys[u, :, columns], (((1,), (1,)), ((), ())), preferred_element_type=F32)
        halved = scores * (0.5 * HEAD_DIM ** (-0.5))
        weight = halved + halved * jnp.tanh(halved)
        kept = jnp.concatenate(
            [(weight * live[u * tiles + t]).astype(BF16) for t in range(tiles)], axis=0)
        sums = jnp.dot(kept, vals[u, :, columns], preferred_element_type=F32)
        both = []
        for t in range(tiles):
            at = t * 2 * item_count
            both.append(jnp.concatenate([
                sums[at : at + item_count, :HEAD_DIM],
                sums[at + item_count : at + 2 * item_count, HEAD_DIM:]], axis=1))
        part[u, p] = jnp.dot(
            chooser[u], jnp.concatenate(both, axis=0).astype(BF16),
            preferred_element_type=F32).astype(BF16)

        @pl.when(p != x)
        def _():
            part_copy(u, p).start()

    def rows_z(at):
        return pl.ds(pl.multiple_of(at * z_rows, z_rows), z_rows)

    def half_copy(u, j):
        to = z_at(j)
        return push(half.at[u, rows_z(to)], half_in.at[u, z], rz_s.at[u * ZS + j], rz_r.at[u * ZS + j],
                    x * ZS + to)

    def reduce_x(u):
        total = part[u, x].astype(F32)
        for j in range(1, XS):
            come = part_in.at[u, x_at(-j)]
            push(come, come, rx_r.at[u * XS + j], rx_r.at[u * XS + j], me).wait_recv()
            total += part_in[u, x_at(-j)].astype(F32)
        half[u] = total.astype(BF16)
        for j in NEAREST[::-1]:
            half_copy(u, j).start()

    def project(u):
        attended = half[u, rows_z(z)].astype(F32)
        for j in NEAREST:
            come = half_in.at[u, z_at(-j)]
            push(come, come, rz_r.at[u * ZS + j], rz_r.at[u * ZS + j], me).wait_recv()
            attended += half_in[u, z_at(-j)].astype(F32)
        squares = attended * attended
        sq[u] = (squares[:, :HEAD_DIM] + squares[:, HEAD_DIM:]).reshape(XS, each, HEAD_DIM)
        gate = jnp.concatenate([gate_in[i, u] for i in range(HEADS // XS)], axis=1).astype(F32)
        width = 2 * HEAD_DIM
        gain = gain_attn[:, pl.ds(pl.multiple_of(x * width, width), width)]
        added = jnp.dot(
            (attended * gain * gate).astype(BF16), wo[...], preferred_element_type=F32
        ).reshape(XS, each, HEADS * HEAD_DIM)
        middle = HEADS * HEAD_DIM // 2
        proj[u] = jnp.concatenate([added[:, :, :middle], added[:, :, middle:]], axis=1).astype(BF16)
        for j in (2, 1, 3):
            to = x_at(j)
            send(push(proj.at[u, to], proj_in.at[u, x], po_s.at[u * XS + j], po_r.at[u * XS + j],
                      to * ZS + z))
            send(push(sq.at[u, to], sq_in.at[u, x], sq_s.at[u * XS + j], sq_r.at[u * XS + j],
                      to * ZS + z))

    def finish(u):
        squares = sq[u, x]
        projected = proj[u, x].astype(F32)
        for j in (1, 3, 2):
            frm = x_at(-j)
            push(proj_in.at[u, frm], proj_in.at[u, frm], po_r.at[u * XS + j], po_r.at[u * XS + j],
                 me).wait_recv()
            projected += proj_in[u, frm].astype(F32)
            push(sq_in.at[u, frm], sq_in.at[u, frm], sq_r.at[u * XS + j], sq_r.at[u * XS + j],
                 me).wait_recv()
            squares += sq_in[u, frm]
        scale = lax.rsqrt(
            jnp.sum(squares, axis=1, keepdims=True) * (1.0 / (HEADS * HEAD_DIM)) + EPSILON)
        projected = jnp.concatenate([projected[:each], projected[each:]], axis=1)
        return tokens[u * each : (u + 1) * each] + projected * scale

    def step(k, carry):
        attend(k)

        @pl.when((k == 1) & (gate_x == x))
        def _():
            make_gate()

        @pl.when(k == steps - 2)
        def _():
            share_wo()
            reduce_x(0)

        return carry

    lax.fori_loop(0, steps, step, 0)
    for u in range(1, users):
        reduce_x(u)
    for i in range(HEADS // XS):
        frm = x * (HEADS // XS) + i

        @pl.when(frm != z)
        def _():
            push(gate_in.at[i], gate_in.at[i], ga_r.at[i], ga_r.at[i], me).wait_recv()
    loads[6].wait()
    for j in range(1, team):
        come = wo.at[:, share_of(lax.rem(member - j + team, team))]
        push(come, come, wo_tr.at[j], wo_tr.at[j], me).wait_recv()
    for u in range(users):
        project(u)
    rows_out = [finish(u) for u in range(users)]
    out[...] = jnp.concatenate(rows_out, axis=0).astype(BF16)

    for copy in sends:
        copy.wait_send()
    for j in range(1, team):
        share_copy(j).wait_send()

    @pl.when(gate_x != x)
    def _():
        wg_copy.wait_send()

    @pl.when(gate_x == x)
    def _():
        for j in range(1, ZS):
            gate_copy(j).wait_send()

    for u in range(users):
        for j in range(1, XS):
            part_copy(u, x_at(j)).wait_send()
        for j in range(1, ZS):
            half_copy(u, j).wait_send()


def on_device(
    cand_items, item_rows, hist_keys, hist_values, block_mask, hist_lengths,
    gain_in, w_query, w_gate, gain_attn, w_out,
):
    row_count, users = cand_items.shape
    item_count, width = item_rows.shape
    events = hist_keys.shape[1]
    rows = w_query.shape[0]
    own = row_count * users
    tiles = block_mask.shape[1]
    user_rows = XS * ZS * row_count
    team = min(TEAM, lax.axis_size("users"))
    dma = pltpu.SemaphoreType.DMA
    anywhere = pl.BlockSpec(memory_space=pl.ANY)
    vmem = pl.BlockSpec(memory_space=pltpu.VMEM)
    ranked = pl.pallas_call(
        kernel,
        out_shape=jax.ShapeDtypeStruct((own, width), BF16),
        in_specs=[anywhere] * 11,
        out_specs=vmem,
        scratch_shapes=[
            pltpu.VMEM((users, row_count), jnp.int32),
            pltpu.SMEM(block_mask.shape, jnp.int32),
            pltpu.SMEM((users,), jnp.int32),
            pltpu.VMEM((1, width), F32),
            pltpu.VMEM((1, width), F32),
            pltpu.VMEM((item_count, width), BF16),
            pltpu.VMEM((users, events, width), BF16),
            pltpu.VMEM((users, events, width), BF16),
            pltpu.VMEM((item_count, width), BF16),
            pltpu.VMEM((ZS, own, item_count), BF16),
            pltpu.VMEM((XS, own, ZS * own), BF16),
            pltpu.VMEM((users, user_rows, tiles * item_count), BF16),
            pltpu.VMEM((users * tiles, 1, events), F32),
            pltpu.VMEM((own, width), F32),
            pltpu.VMEM((XS * ZS * rows, HEAD_DIM), BF16),
            pltpu.VMEM((XS * ZS * rows, HEAD_DIM), BF16),
            pltpu.VMEM((ZS * rows, width), BF16),
            pltpu.VMEM((HEADS, item_count, HEAD_DIM), BF16),
            pltpu.VMEM((ZS, users, user_rows // ZS, HEAD_DIM), BF16),
            pltpu.VMEM((HEADS // XS, users, user_rows // ZS, HEAD_DIM), BF16),
            pltpu.VMEM((users, XS, user_rows, 2 * HEAD_DIM), BF16),
            pltpu.VMEM((users, XS, user_rows, 2 * HEAD_DIM), BF16),
            pltpu.VMEM((users, user_rows, 2 * HEAD_DIM), BF16),
            pltpu.VMEM((users, ZS, user_rows // ZS, 2 * HEAD_DIM), BF16),
            pltpu.VMEM((users, XS, own, width // 2), BF16),
            pltpu.VMEM((users, XS, own, width // 2), BF16),
            pltpu.VMEM((users, XS, row_count, HEAD_DIM), F32),
            pltpu.VMEM((users, XS, row_count, HEAD_DIM), F32),
            dma((9 + 2 * users,)),
            dma((ZS,)), dma((ZS,)), dma((XS,)), dma((XS,)),
            dma((ZS,)), dma((ZS,)), dma((XS,)), dma((XS,)),
            dma((ZS,)), dma((ZS,)), dma((XS,)), dma((XS,)),
            dma((ZS,)), dma((ZS,)), dma((team,)), dma((team,)),
            dma((ZS,)), dma((ZS,)),
            dma((ZS,)), dma((HEADS // XS,)),
            dma((users * XS,)), dma((users * XS,)),
            dma((users * ZS,)), dma((users * ZS,)),
            dma((users * XS,)), dma((users * XS,)),
            dma((users * XS,)), dma((users * XS,)),
        ],
        compiler_params=pltpu.CompilerParams(
            collective_id=0, has_side_effects=True, vmem_limit_bytes=63 * 1024 * 1024),
        cost_estimate=pl.CostEstimate(flops=10**9, bytes_accessed=5 * 10**6, transcendentals=10**6),
        name="ranked",
    )(
        cand_items.T, item_rows, hist_keys, hist_values, block_mask, hist_lengths,
        gain_in.reshape(1, width), w_query, w_gate, gain_attn.reshape(1, width), w_out,
    )
    return ranked.reshape(users, row_count, width).transpose(1, 0, 2)


def solution(mesh):
    in_specs = (
        P(("users", "seq"), None),
        P("users", None),
        P("users", "seq", None),
        P("users", "seq", None),
        P("users", None, "seq"),
        P("users"),
        P(),
        P("seq", None),
        P("seq", None),
        P(),
        P("seq", None),
    )
    out_specs = P(("users", "seq"), None, None)
    return jax.shard_map(
        on_device, mesh=mesh, in_specs=in_specs, out_specs=out_specs, check_vma=False
    )
```

time: 59.4 us -> 53.5 us (0.901)
  Pallas kernels: 57.7 us -> 51.6 us
    pallas_call x1, Pallas kernels: 57.7 us -> 51.6 us  [on_device(): pl.pallas_call(kernel, out_shape=jax.ShapeDtypeStruct((own, width), BF16)...]
where the time goes in v2:
time: 53.5 us; the launch traced here: 53 us
  Pallas kernels  51.6 us (96%)
  local copies, waits for them, and re-layouts  1.41 us (3%)
    pallas_call x1, Pallas kernels, on_device(): pl.pallas_call(kernel, out_shape=jax.ShapeDtypeStruct((own, width), BF16)...  51.6 us
    reshape x1, local copies, waits for them, and re-layouts, on_device(): return ranked.reshape(users, row_count, width).transpose(1, 0, 2)  1.41 us

profile of v2, /device:TPU:56, one launch (start us, length us, event | category | flops | bytes accessed | tf_op | source)
XLA Modules:
  0.0 53.0 jit_solution(12090256336462032611)
XLA Ops:
  0.0 51.6 %ranked.1 = bf16[16,1024]{1,0:T(8,128)(2,1)} custom-call(s32[2,8]{1,0:T(2,128)} %bitcast.10, bf16[128,1024]{1,0:T(8,128)(2,1)} %items_hbm.1, bf16[2,512,1024]{2,1,0:T(8,128)(2,1)} %keys_hbm.1, bf16[2,512,1024]{2,1,0:T(8,128)(2,1)} %vals_hbm.1, s32[2,2,4]{2,1,0:T(2,128)} %mask_hbm.1, s32[2]{0:T(128)} %lens_hbm.1, f32[1,1024]{1,0:T(1,128)} %bitcast.8, ...), custom_call_target="tpu_custom_call" | custom-call | flops 1000000000 | bytes 5000000 | tf_op jit(solution)/shard_map/ranked/pallas_call | solution.py:427
  51.6 1.4 %copy.14 = bf16[2,8,1024]{2,0,1:T(2,128)(2,1)} copy(bf16[2,8,1024]{2,1,0:T(8,128)(2,1)} %bitcast.7) | data formatting | bytes 65536 | tf_op jit(solution)/shard_map/reshape | solution.py:481

commit v3 on v2

--- a/solution.py
+++ b/solution.py
@@ -31,9 +31,9 @@
     gain_attn_hbm, wo_hbm,
     out,
     cand, mask, lens, gain_in, gain_attn, items, keys, vals, normed, picks, ids_x, chooser, live,
-    tokens, wq, wg, wo, query, gate_out, gate_in, part, part_in, half, half_in, proj, proj_in, sq, sq_in,
+    tokens, wq, wg, wo, query, gate_out, gate_in, part, relay, part_in, half, half_in, proj, proj_in, sq, sq_in,
     load_sem, wq_zs, wq_zr, wq_xs, wq_xr, wg_zs, wg_zr, wg_xs, wg_xr, oh_zs, oh_zr, oh_xs, oh_xr,
-    wo_zs, wo_zr, wo_ts, wo_tr, q_s, q_r, ga_s, ga_r, rx_s, rx_r, rz_s, rz_r, po_s, po_r, sq_s, sq_r,
+    wo_zs, wo_zr, wo_ts, wo_tr, q_s, q_r, ga_s, ga_r, rl_s, rl_r, rx_s, rx_r, rz_s, rz_r, po_s, po_r, sq_s, sq_r,
 ):
     me = lax.axis_index("seq")
     x, z = lax.div(me, ZS), lax.rem(me, ZS)
@@ -179,18 +179,22 @@
     wg_copy = push(wg.at[group(x)], wg.at[group(x)], wg_xs.at[gate_step], wg_xr.at[gate_step],
                    gate_x * ZS + z)
     slot = lax.rem(z, HEADS // XS)
-    loads[4].wait()
-    for j in range(1, ZS):
-        come = wg.at[rows_of(x * ZS + z_at(-j))]
-        push(come, come, wg_zr.at[j], wg_zr.at[j], me).wait_recv()
-
-    @pl.when(gate_x != x)
-    def _():
-        wg_copy.start()
-
-    for j in range(1, ZS):
-        send(push(wo_hbm.at[:, share_of(member)], wo.at[rows_of(z), share_of(member)],
-                  wo_zs.at[j], wo_zr.at[j], x * ZS + z_at(j)))
+    def share_part(j):
+        return push(wo_hbm.at[:, share_of(member)], wo.at[rows_of(z), share_of(member)],
+                    wo_zs.at[j], wo_zr.at[j], x * ZS + z_at(j))
+
+    def pass_weights():
+        loads[4].wait()
+        for j in range(1, ZS):
+            come = wg.at[rows_of(x * ZS + z_at(-j))]
+            push(come, come, wg_zr.at[j], wg_zr.at[j], me).wait_recv()
+
+        @pl.when(gate_x != x)
+        def _():
+            wg_copy.start()
+
+        for j in range(1, ZS):
+            share_part(j).start()
 
     def share_copy(j):
         return pltpu.make_async_remote_copy(
@@ -250,6 +254,7 @@
 
     pairs = HEADS // 2
     steps = users * pairs
+    lag = 2
 
     def place_of(k):
         u, s = lax.div(k, pairs), lax.rem(k, pairs)
@@ -295,9 +300,46 @@
             chooser[u], jnp.concatenate(both, axis=0).astype(BF16),
             preferred_element_type=F32).astype(BF16)
 
-        @pl.when(p != x)
+        @pl.when((u > 0) & (p != x))
         def _():
             part_copy(u, p).start()
+
+        role = lax.rem(x - p + XS, XS)
+
+        @pl.when((u == 0) & (role == 2))
+        def _():
+            relay_copy(0).start()
+            relay_copy(1).start()
+
+        @pl.when((u == 0) & (role == 1))
+        def _():
+            near_copy(0, 1).start()
+
+        @pl.when((u == 0) & (role == 3))
+        def _():
+            near_copy(1, 0).start()
+
+    sides = (x_at(-1), x_at(1))
+    middle_row = chooser.shape[1] // 2
+    halves = (pl.ds(0, middle_row), pl.ds(middle_row, middle_row))
+
+    def relay_copy(i):
+        return push(part.at[0, x_at(2), halves[i]], relay.at[i], rl_s.at[i], rl_r.at[i],
+                    sides[i] * ZS + z)
+
+    def near_copy(side, i):
+        return push(part.at[0, sides[side], halves[i]], part_in.at[0, side, halves[i]],
+                    rx_s.at[side * 2 + i], rx_r.at[side * 2 + i], sides[side] * ZS + z)
+
+    def pass_on(k):
+        u, p = place_of(k)
+        for i in range(2):
+            @pl.when(p == sides[i])
+            def _():
+                relay_copy(i).wait_recv()
+                part[0, p, halves[i]] = (
+                    part[0, p, halves[i]].astype(F32) + relay[i].astype(F32)).astype(BF16)
+                near_copy(i, i).start()
 
     def rows_z(at):
         return pl.ds(pl.multiple_of(at * z_rows, z_rows), z_rows)
@@ -309,10 +351,16 @@
 
     def reduce_x(u):
         total = part[u, x].astype(F32)
-        for j in range(1, XS):
-            come = part_in.at[u, x_at(-j)]
-            push(come, come, rx_r.at[u * XS + j], rx_r.at[u * XS + j], me).wait_recv()
-            total += part_in[u, x_at(-j)].astype(F32)
+        if u == 0:
+            for side in range(2):
+                for i in range(2):
+                    near_copy(side, i).wait_recv()
+                total += part_in[0, side].astype(F32)
+        else:
+            for j in range(1, XS):
+                come = part_in.at[u, x_at(-j)]
+                push(come, come, rx_r.at[u * XS + j], rx_r.at[u * XS + j], me).wait_recv()
+                total += part_in[u, x_at(-j)].astype(F32)
         half[u] = total.astype(BF16)
         for j in NEAREST[::-1]:
             half_copy(u, j).start()
@@ -359,9 +407,17 @@
     def step(k, carry):
         attend(k)
 
-        @pl.when((k == 1) & (gate_x == x))
+        @pl.when(k == 0)
+        def _():
+            pass_weights()
+
+        @pl.when((k == 2) & (gate_x == x))
         def _():
             make_gate()
+
+        @pl.when((k >= lag) & (k < pairs + lag))
+        def _():
+            pass_on(k - lag)
 
         @pl.when(k == steps - 2)
         def _():
@@ -383,9 +439,10 @@
     for j in range(1, team):
         come = wo.at[:, share_of(lax.rem(member - j + team, team))]
         push(come, come, wo_tr.at[j], wo_tr.at[j], me).wait_recv()
+    rows_out = []
     for u in range(users):
         project(u)
-    rows_out = [finish(u) for u in range(users)]
+        rows_out.append(finish(u))
     out[...] = jnp.concatenate(rows_out, axis=0).astype(BF16)
 
     for copy in sends:
@@ -402,8 +459,14 @@
         for j in range(1, ZS):
             gate_copy(j).wait_send()
 
+    for j in range(1, ZS):
+        share_part(j).wait_send()
+    for i in range(2):
+        relay_copy(i).wait_send()
+        for side in range(2):
+            near_copy(side, i).wait_send()
     for u in range(users):
-        for j in range(1, XS):
+        for j in range(1, XS if u > 0 else 1):
             part_copy(u, x_at(j)).wait_send()
         for j in range(1, ZS):
             half_copy(u, j).wait_send()
@@ -451,6 +514,7 @@
             pltpu.VMEM((ZS, users, user_rows // ZS, HEAD_DIM), BF16),
             pltpu.VMEM((HEADS // XS, users, user_rows // ZS, HEAD_DIM), BF16),
             pltpu.VMEM((users, XS, user_rows, 2 * HEAD_DIM), BF16),
+            pltpu.VMEM((2, user_rows // 2, 2 * HEAD_DIM), BF16),
             pltpu.VMEM((users, XS, user_rows, 2 * HEAD_DIM), BF16),
             pltpu.VMEM((users, user_rows, 2 * HEAD_DIM), BF16),
             pltpu.VMEM((users, ZS, user_rows // ZS, 2 * HEAD_DIM), BF16),
@@ -465,6 +529,7 @@
             dma((ZS,)), dma((ZS,)), dma((team,)), dma((team,)),
             dma((ZS,)), dma((ZS,)),
             dma((ZS,)), dma((HEADS // XS,)),
+            dma((2,)), dma((2,)),
             dma((users * XS,)), dma((users * XS,)),
             dma((users * ZS,)), dma((users * ZS,)),
             dma((users * XS,)), dma((users * XS,)),

time: 53.5 us -> 58.6 us (1.095)
  Pallas kernels: 51.6 us -> 56.8 us
    pallas_call x1, Pallas kernels: 51.6 us -> 56.8 us  [on_device(): pl.pallas_call(kernel, out_shape=jax.ShapeDtypeStruct((own, width), BF16)...]
where the time goes in v3:
time: 58.6 us; the launch traced here: 58.2 us
  Pallas kernels  56.8 us (97%)
  local copies, waits for them, and re-layouts  1.41 us (2%)
    pallas_call x1, Pallas kernels, on_device(): pl.pallas_call(kernel, out_shape=jax.ShapeDtypeStruct((own, width), BF16)...  56.8 us
    reshape x1, local copies, waits for them, and re-layouts, on_device(): return ranked.reshape(users, row_count, width).transpose(1, 0, 2)  1.41 us

profile of v3, /device:TPU:56, one launch (start us, length us, event | category | flops | bytes accessed | tf_op | source)
XLA Modules:
  0.0 58.2 jit_solution(10888620572270657013)
XLA Ops:
  0.0 56.8 %ranked.1 = bf16[16,1024]{1,0:T(8,128)(2,1)} custom-call(s32[2,8]{1,0:T(2,128)} %bitcast.10, bf16[128,1024]{1,0:T(8,128)(2,1)} %items_hbm.1, bf16[2,512,1024]{2,1,0:T(8,128)(2,1)} %keys_hbm.1, bf16[2,512,1024]{2,1,0:T(8,128)(2,1)} %vals_hbm.1, s32[2,2,4]{2,1,0:T(2,128)} %mask_hbm.1, s32[2]{0:T(128)} %lens_hbm.1, f32[1,1024]{1,0:T(1,128)} %bitcast.8, ...), custom_call_target="tpu_custom_call" | custom-call | flops 1000000000 | bytes 5000000 | tf_op jit(solution)/shard_map/ranked/pallas_call | solution.py:490
  56.8 1.4 %copy.14 = bf16[2,8,1024]{2,0,1:T(2,128)(2,1)} copy(bf16[2,8,1024]{2,1,0:T(8,128)(2,1)} %bitcast.7) | data formatting | bytes 65536 | tf_op jit(solution)/shard_map/reshape | solution.py:546

commit v4 on v2

--- a/solution.py
+++ b/solution.py
@@ -145,6 +145,10 @@
         send(push(wg_hbm.at[:, lanes(to)], wg.at[rows_of(me)], wg_zs.at[j], wg_zr.at[j], x * ZS + to))
 
     for j in range(1, ZS):
+        send(push(wo_hbm.at[:, share_of(member)], wo.at[rows_of(z), share_of(member)],
+                  wo_zs.at[j], wo_zr.at[j], x * ZS + z_at(j)))
+
+    for j in range(1, ZS):
         come = picks.at[z_at(-j)]
         push(come, come, oh_zr.at[j], oh_zr.at[j], me).wait_recv()
     group_rows = ZS * own
@@ -187,10 +191,6 @@
     @pl.when(gate_x != x)
     def _():
         wg_copy.start()
-
-    for j in range(1, ZS):
-        send(push(wo_hbm.at[:, share_of(member)], wo.at[rows_of(z), share_of(member)],
-                  wo_zs.at[j], wo_zr.at[j], x * ZS + z_at(j)))
 
     def share_copy(j):
         return pltpu.make_async_remote_copy(
@@ -359,18 +359,22 @@
     def step(k, carry):
         attend(k)
 
-        @pl.when((k == 1) & (gate_x == x))
+        @pl.when(k == 2)
         def _():
-            make_gate()
+            share_wo()
 
         @pl.when(k == steps - 2)
         def _():
-            share_wo()
             reduce_x(0)
 
         return carry
 
     lax.fori_loop(0, steps, step, 0)
+
+    @pl.when(gate_x == x)
+    def _():
+        make_gate()
+
     for u in range(1, users):
         reduce_x(u)
     for i in range(HEADS // XS):
@@ -383,9 +387,10 @@
     for j in range(1, team):
         come = wo.at[:, share_of(lax.rem(member - j + team, team))]
         push(come, come, wo_tr.at[j], wo_tr.at[j], me).wait_recv()
+    rows_out = []
     for u in range(users):
         project(u)
-    rows_out = [finish(u) for u in range(users)]
+        rows_out.append(finish(u))
     out[...] = jnp.concatenate(rows_out, axis=0).astype(BF16)
 
     for copy in sends:

time: 53.5 us -> 57 us (1.065)
  Pallas kernels: 51.6 us -> 55 us
    pallas_call x1, Pallas kernels: 51.6 us -> 55 us  [on_device(): pl.pallas_call(kernel, out_shape=jax.ShapeDtypeStruct((own, width), BF16)...]
where the time goes in v4:
time: 57 us; the launch traced here: 56.4 us
  Pallas kernels  55 us (96%)
  local copies, waits for them, and re-layouts  1.41 us (2%)
    pallas_call x1, Pallas kernels, on_device(): pl.pallas_call(kernel, out_shape=jax.ShapeDtypeStruct((own, width), BF16)...  55 us
    reshape x1, local copies, waits for them, and re-layouts, on_device(): return ranked.reshape(users, row_count, width).transpose(1, 0, 2)  1.41 us

profile of v4, /device:TPU:56, one launch (start us, length us, event | category | flops | bytes accessed | tf_op | source)
XLA Modules:
  0.0 56.4 jit_solution(14756182562202621572)
XLA Ops:
  0.0 55.0 %ranked.1 = bf16[16,1024]{1,0:T(8,128)(2,1)} custom-call(s32[2,8]{1,0:T(2,128)} %bitcast.10, bf16[128,1024]{1,0:T(8,128)(2,1)} %items_hbm.1, bf16[2,512,1024]{2,1,0:T(8,128)(2,1)} %keys_hbm.1, bf16[2,512,1024]{2,1,0:T(8,128)(2,1)} %vals_hbm.1, s32[2,2,4]{2,1,0:T(2,128)} %mask_hbm.1, s32[2]{0:T(128)} %lens_hbm.1, f32[1,1024]{1,0:T(1,128)} %bitcast.8, ...), custom_call_target="tpu_custom_call" | custom-call | flops 1000000000 | bytes 5000000 | tf_op jit(solution)/shard_map/ranked/pallas_call | solution.py:432
  55.0 1.4 %copy.14 = bf16[2,8,1024]{2,0,1:T(2,128)(2,1)} copy(bf16[2,8,1024]{2,1,0:T(8,128)(2,1)} %bitcast.7) | data formatting | bytes 65536 | tf_op jit(solution)/shard_map/reshape | solution.py:486

commit v5 on v2

--- a/solution.py
+++ b/solution.py
@@ -31,7 +31,7 @@
     gain_attn_hbm, wo_hbm,
     out,
     cand, mask, lens, gain_in, gain_attn, items, keys, vals, normed, picks, ids_x, chooser, live,
-    tokens, wq, wg, wo, query, gate_out, gate_in, part, part_in, half, half_in, proj, proj_in, sq, sq_in,
+    tokens, wq, query_part, wg, wo, query, gate_out, gate_in, part, part_in, half, half_in, proj, proj_in, sq, sq_in,
     load_sem, wq_zs, wq_zr, wq_xs, wq_xr, wg_zs, wg_zr, wg_xs, wg_xr, oh_zs, oh_zr, oh_xs, oh_xr,
     wo_zs, wo_zr, wo_ts, wo_tr, q_s, q_r, ga_s, ga_r, rx_s, rx_r, rz_s, rz_r, po_s, po_r, sq_s, sq_r,
 ):
@@ -137,8 +137,13 @@
     for j in range(1, ZS):
         come = wq.at[rows_of(x * ZS + z_at(-j))]
         push(come, come, wq_zr.at[j], wq_zr.at[j], me).wait_recv()
+    depth = ZS * rows
+    own_part = jnp.dot(
+        normed[:, pl.ds(pl.multiple_of(x * depth, depth), depth)], wq[group(x)],
+        preferred_element_type=F32)
+    query_part[x] = own_part.astype(BF16)
     for j in range(1, XS):
-        send(push(wq.at[group(x)], wq.at[group(x)], wq_xs.at[j], wq_xr.at[j], x_at(j) * ZS + z))
+        send(push(query_part.at[x], query_part.at[x], wq_xs.at[j], wq_xr.at[j], x_at(j) * ZS + z))
 
     for j in range(1, ZS):
         to = z_at(j)
@@ -167,10 +172,12 @@
                 live[u * tiles + t, :, pl.ds(b * BLOCK, BLOCK)] = jnp.where(
                     (opened == 1) & (place < length), 1.0, 0.0)
 
+    asked_z = own_part
     for j in range(1, XS):
-        come = wq.at[group(x_at(-j))]
+        come = query_part.at[x_at(-j)]
         push(come, come, wq_xr.at[j], wq_xr.at[j], me).wait_recv()
-    query[z] = silu(jnp.dot(normed[...], wq[...], preferred_element_type=F32)).astype(BF16)
+        asked_z += query_part[x_at(-j)].astype(F32)
+    query[z] = silu(asked_z).astype(BF16)
     for j in NEAREST:
         send(push(query.at[z], query.at[z], q_s.at[j], q_r.at[j], x * ZS + z_at(j)))
 
@@ -365,8 +372,8 @@
 
         @pl.when(k == steps - 2)
         def _():
+            reduce_x(0)
             share_wo()
-            reduce_x(0)
 
         return carry
 
@@ -445,6 +452,7 @@
             pltpu.VMEM((users * tiles, 1, events), F32),
             pltpu.VMEM((own, width), F32),
             pltpu.VMEM((XS * ZS * rows, HEAD_DIM), BF16),
+            pltpu.VMEM((XS, item_count, HEAD_DIM), BF16),
             pltpu.VMEM((XS * ZS * rows, HEAD_DIM), BF16),
             pltpu.VMEM((ZS * rows, width), BF16),
             pltpu.VMEM((HEADS, item_count, HEAD_DIM), BF16),

time: 53.5 us -> 52.7 us (0.985)
  Pallas kernels: 51.6 us -> 50.8 us
    pallas_call x1, Pallas kernels: 51.6 us -> 50.8 us  [on_device(): pl.pallas_call(kernel, out_shape=jax.ShapeDtypeStruct((own, width), BF16)...]
where the time goes in v5:
time: 52.7 us; the launch traced here: 52.2 us
  Pallas kernels  50.8 us (96%)
  local copies, waits for them, and re-layouts  1.41 us (3%)
    pallas_call x1, Pallas kernels, on_device(): pl.pallas_call(kernel, out_shape=jax.ShapeDtypeStruct((own, width), BF16)...  50.8 us
    reshape x1, local copies, waits for them, and re-layouts, on_device(): return ranked.reshape(users, row_count, width).transpose(1, 0, 2)  1.41 us

profile of v5, /device:TPU:56, one launch (start us, length us, event | category | flops | bytes accessed | tf_op | source)
XLA Modules:
  0.0 52.2 jit_solution(3778338509561094904)
XLA Ops:
  0.0 50.8 %ranked.1 = bf16[16,1024]{1,0:T(8,128)(2,1)} custom-call(s32[2,8]{1,0:T(2,128)} %bitcast.10, bf16[128,1024]{1,0:T(8,128)(2,1)} %items_hbm.1, bf16[2,512,1024]{2,1,0:T(8,128)(2,1)} %keys_hbm.1, bf16[2,512,1024]{2,1,0:T(8,128)(2,1)} %vals_hbm.1, s32[2,2,4]{2,1,0:T(2,128)} %mask_hbm.1, s32[2]{0:T(128)} %lens_hbm.1, f32[1,1024]{1,0:T(1,128)} %bitcast.8, ...), custom_call_target="tpu_custom_call" | custom-call | flops 1000000000 | bytes 5000000 | tf_op jit(solution)/shard_map/ranked/pallas_call | solution.py:434
  50.8 1.4 %copy.14 = bf16[2,8,1024]{2,0,1:T(2,128)(2,1)} copy(bf16[2,8,1024]{2,1,0:T(8,128)(2,1)} %bitcast.7) | data formatting | bytes 65536 | tf_op jit(solution)/shard_map/reshape | solution.py:489

commit v6 on v5

--- a/solution.py
+++ b/solution.py
@@ -11,7 +11,7 @@
 EPSILON = 1e-06
 XS, ZS = 4, 8
 NEAREST = (7, 1, 6, 2, 5, 3, 4)
-TEAM = 4
+TEAM = 2
 MESH = pl.DeviceIdType.MESH
 BF16, F32 = jnp.bfloat16, jnp.float32
 

time: 52.7 us -> 53.6 us (1.017)
  Pallas kernels: 50.8 us -> 51.7 us
    pallas_call x1, Pallas kernels: 50.8 us -> 51.7 us  [on_device(): pl.pallas_call(kernel, out_shape=jax.ShapeDtypeStruct((own, width), BF16)...]
where the time goes in v6:
time: 53.6 us; the launch traced here: 53.2 us
  Pallas kernels  51.7 us (96%)
  local copies, waits for them, and re-layouts  1.41 us (3%)
    pallas_call x1, Pallas kernels, on_device(): pl.pallas_call(kernel, out_shape=jax.ShapeDtypeStruct((own, width), BF16)...  51.7 us
    reshape x1, local copies, waits for them, and re-layouts, on_device(): return ranked.reshape(users, row_count, width).transpose(1, 0, 2)  1.41 us

profile of v6, /device:TPU:56, one launch (start us, length us, event | category | flops | bytes accessed | tf_op | source)
XLA Modules:
  0.0 53.2 jit_solution(8380148293237559909)
XLA Ops:
  0.0 51.7 %ranked.1 = bf16[16,1024]{1,0:T(8,128)(2,1)} custom-call(s32[2,8]{1,0:T(2,128)} %bitcast.10, bf16[128,1024]{1,0:T(8,128)(2,1)} %items_hbm.1, bf16[2,512,1024]{2,1,0:T(8,128)(2,1)} %keys_hbm.1, bf16[2,512,1024]{2,1,0:T(8,128)(2,1)} %vals_hbm.1, s32[2,2,4]{2,1,0:T(2,128)} %mask_hbm.1, s32[2]{0:T(128)} %lens_hbm.1, f32[1,1024]{1,0:T(1,128)} %bitcast.8, ...), custom_call_target="tpu_custom_call" | custom-call | flops 1000000000 | bytes 5000000 | tf_op jit(solution)/shard_map/ranked/pallas_call | solution.py:434
  51.7 1.4 %copy.14 = bf16[2,8,1024]{2,0,1:T(2,128)(2,1)} copy(bf16[2,8,1024]{2,1,0:T(8,128)(2,1)} %bitcast.7) | data formatting | bytes 65536 | tf_op jit(solution)/shard_map/reshape | solution.py:489

commit v7 on v5

--- a/solution.py
+++ b/solution.py
@@ -390,9 +390,10 @@
     for j in range(1, team):
         come = wo.at[:, share_of(lax.rem(member - j + team, team))]
         push(come, come, wo_tr.at[j], wo_tr.at[j], me).wait_recv()
+    rows_out = []
     for u in range(users):
         project(u)
-    rows_out = [finish(u) for u in range(users)]
+        rows_out.append(finish(u))
     out[...] = jnp.concatenate(rows_out, axis=0).astype(BF16)
 
     for copy in sends:

time: 52.7 us -> 54.9 us (1.042)
  Pallas kernels: 50.8 us -> 53.3 us
    pallas_call x1, Pallas kernels: 50.8 us -> 53.3 us  [on_device(): pl.pallas_call(kernel, out_shape=jax.ShapeDtypeStruct((own, width), BF16)...]
where the time goes in v7:
time: 54.9 us; the launch traced here: 54.8 us
  Pallas kernels  53.3 us (97%)
  local copies, waits for them, and re-layouts  1.41 us (3%)
    pallas_call x1, Pallas kernels, on_device(): pl.pallas_call(kernel, out_shape=jax.ShapeDtypeStruct((own, width), BF16)...  53.3 us
    reshape x1, local copies, waits for them, and re-layouts, on_device(): return ranked.reshape(users, row_count, width).transpose(1, 0, 2)  1.41 us

profile of v7, /device:TPU:56, one launch (start us, length us, event | category | flops | bytes accessed | tf_op | source)
XLA Modules:
  0.0 54.8 jit_solution(13221863392754848621)
XLA Ops:
  0.0 53.3 %ranked.1 = bf16[16,1024]{1,0:T(8,128)(2,1)} custom-call(s32[2,8]{1,0:T(2,128)} %bitcast.10, bf16[128,1024]{1,0:T(8,128)(2,1)} %items_hbm.1, bf16[2,512,1024]{2,1,0:T(8,128)(2,1)} %keys_hbm.1, bf16[2,512,1024]{2,1,0:T(8,128)(2,1)} %vals_hbm.1, s32[2,2,4]{2,1,0:T(2,128)} %mask_hbm.1, s32[2]{0:T(128)} %lens_hbm.1, f32[1,1024]{1,0:T(1,128)} %bitcast.8, ...), custom_call_target="tpu_custom_call" | custom-call | flops 1000000000 | bytes 5000000 | tf_op jit(solution)/shard_map/ranked/pallas_call | solution.py:435
  53.4 1.4 %copy.14 = bf16[2,8,1024]{2,0,1:T(2,128)(2,1)} copy(bf16[2,8,1024]{2,1,0:T(8,128)(2,1)} %bitcast.7) | data formatting | bytes 65536 | tf_op jit(solution)/shard_map/reshape | solution.py:490
